TPU v7x, 32 devices: a whole 2x2x4 slice. The times are simulated.
32 devices in a mesh: dp: 8 (over z, y), blk: 4 (over x, core).
Axes of the slice: x: 2, y: 2, z: 4, core: 2. Of those that a mesh axis runs over, the one named last changes fastest.
Arguments:
- long_input: bfloat16 [24, 512, 768], P('dp', 'blk'), may hold values from -6 to 6
- short_input: bfloat16 [8, 4, 8, 128, 768], P('dp', 'blk'), may hold values from -6 to 6
- long_cotan: bfloat16 [24, 512, 768], P('dp', 'blk'), may hold values from -6 to 6
- short_cotan: bfloat16 [8, 4, 8, 128, 768], P('dp', 'blk'), may hold values from -6 to 6
- live_slots: int32 [8, 4], P('dp', 'blk'), may hold values from 1 to 8, as said below
- w_project: bfloat16 [768, 1152], replicated, may hold values from -0.3125 to 0.3125
- bias_query: bfloat16 [384], replicated, may hold values from -3 to 3
- bias_value: bfloat16 [384], replicated, may hold values from -3 to 3
- depth_kernel: bfloat16 [9, 768], replicated, may hold values from -2 to 2
- w_point: bfloat16 [768, 384], replicated, may hold values from -0.21875 to 0.21875
- bias_point: bfloat16 [384], replicated, may hold values from -3 to 3
- w_span: bfloat16 [384, 54], replicated, may hold values from -0.3125 to 0.3125
- bias_span: bfloat16 [54], replicated, may hold values from -3 to 3
- w_unfold: bfloat16 [768, 384], replicated, may hold values from -0.21875 to 0.21875
- bias_unfold: bfloat16 [384], replicated, may hold values from -3 to 3
- w_output: bfloat16 [768, 768], replicated, may hold values from -0.875 to 0.875
- bias_output: bfloat16 [768], replicated, may hold values from -3 to 3
- gain_first: bfloat16 [768], replicated, may hold values from 0.25 to 1.75
- shift_first: bfloat16 [768], replicated, may hold values from -2 to 2
- w_inner: bfloat16 [2, 384, 1536], replicated, may hold values from -0.3125 to 0.3125
- bias_inner: bfloat16 [3072], replicated, may hold values from -3 to 3
- w_outer: bfloat16 [2, 1536, 384], replicated, may hold values from -0.15625 to 0.15625
- bias_outer: bfloat16 [768], replicated, may hold values from -3 to 3
- gain_second: bfloat16 [768], replicated, may hold values from 0.25 to 1.75
- shift_second: bfloat16 [768], replicated, may hold values from -2 to 2
Outputs:
- long_output: bfloat16 [24, 512, 768], P('dp', 'blk')
- short_output: bfloat16 [8, 4, 8, 128, 768], P('dp', 'blk')
- long_grad: float32 [24, 512, 768], P('dp', 'blk')
- short_grad: float32 [8, 4, 8, 128, 768], P('dp', 'blk')
- w_project_grad: float32 [768, 1152], replicated
- bias_query_grad: float32 [384], replicated
- bias_value_grad: float32 [384], replicated
- depth_kernel_grad: float32 [9, 768], replicated
- w_point_grad: float32 [768, 384], replicated
- bias_point_grad: float32 [384], replicated
- w_span_grad: float32 [384, 54], replicated
- bias_span_grad: float32 [54], replicated
- w_unfold_grad: float32 [768, 384], replicated
- bias_unfold_grad: float32 [384], replicated
- w_output_grad: float32 [768, 768], replicated
- bias_output_grad: float32 [768], replicated
- gain_first_grad: float32 [768], replicated
- shift_first_grad: float32 [768], replicated
- w_inner_grad: float32 [2, 384, 1536], replicated
- bias_inner_grad: float32 [3072], replicated
- w_outer_grad: float32 [2, 1536, 384], replicated
- bias_outer_grad: float32 [768], replicated
- gain_second_grad: float32 [768], replicated
- shift_second_grad: float32 [768], replicated
Inputs may be any that keep to these rules, and one draw needn't show every extreme that they name: Device (i, j) uses its short row slots 0 to live_slots[i, j] - 1; in every draw some device uses all 8.
All inputs are finite; a program needn't handle non-finite values.
Results may differ from a plain program's by a relative error of at most 0.014.
The roundings to bfloat16 on the way count: a program that leaves them out, or rounds other values in their place, can miss the bound.
Values may be sent and summed in bfloat16 or wider, within the bound.
A program may use at most 192 MiB of HBM per device.

v0:
```python
import functools

import jax
import jax.numpy as jnp
import numpy as np
from jax import lax
from jax.experimental import pallas as pl
from jax.experimental.pallas import tpu as pltpu
from jax.sharding import PartitionSpec as P

D = 768
FF = 3072
HEADS = 6
HEAD = 64
KERNEL = 9
GROUPS = 2
ALL = 384
PAIRS = 3
TAPS = HEADS * KERNEL
HALF = KERNEL // 2

F32 = jnp.float32
BF = jnp.bfloat16
ROOT_HALF = 0.7071067811865476
DENSITY = 0.3989422804014327
FFN_ROWS = 256
FFN_LONG = 384
SHORT_BATCH = 2
LONG_BATCH = 1
VMEM = {
    "pre_short": 58,
    "pre_long": 36,
    "ffn_short": 42,
    "ffn_long": 46,
    "post_short": 46,
    "post_long": 34,
    "end": 34,
    "weights": 48,
    "unpack": 48,
}


def nn(a, b):
    return lax.dot_general(a, b, (((1,), (0,)), ((), ())), preferred_element_type=F32)


def nt(a, b):
    return lax.dot_general(a, b, (((1,), (1,)), ((), ())), preferred_element_type=F32)


def tn(a, b):
    return lax.dot_general(a, b, (((0,), (0,)), ((), ())), preferred_element_type=F32)


def tap_tables():
    perm = np.zeros((128, 128), np.float32)
    spread = np.zeros((256, PAIRS * KERNEL * 128), np.float32)
    for h in range(HEADS):
        for j in range(KERNEL):
            lane = j * HEADS + h
            perm[h * KERNEL + j, lane] = 1
            perm[h * KERNEL + j, TAPS + lane] = 1
            start = ((h // 2) * KERNEL + j) * 128 + (h % 2) * HEAD
            spread[lane, start : start + HEAD] = 1
            spread[128 + lane, start : start + HEAD] = 1
    return perm.astype(jnp.bfloat16), spread.astype(jnp.bfloat16)


def window(values, op):
    left = lambda v, n: pltpu.roll(v, 128 - n, 1)
    one = op(values, left(values, 6))
    two = op(one, left(one, 12))
    four = op(two, left(two, 24))
    return op(four, left(values, 48))


def window_sum(values):
    return window(values + pltpu.roll(values, TAPS, 1), jnp.add)


def head_stack(rows, low_half):
    zero = jnp.zeros_like(rows)
    return jnp.concatenate(
        [jnp.where(low_half, rows, zero), jnp.where(low_half, zero, rows)], axis=0
    )


def two_parts(values):
    high = values.astype(BF)
    rest = (values - high.astype(F32)).astype(BF)
    return jnp.concatenate([high, rest], axis=1)


def row_sides():
    place = lax.axis_index("blk")
    count = lax.axis_size("blk")
    return (place > 0).astype(F32), (place < count - 1).astype(F32), lax.rem(place, 2) == 1


def pick(odd, first, second):
    return jnp.where(odd, first.astype(F32), second.astype(F32))


def row_ends(x_refs, r, sides):
    lower, upper, odd = sides
    rows = x_refs[0].shape[1]
    before = pick(odd, x_refs[1][r, rows - 16 :, :], x_refs[3][r, rows - 16 :, :])
    after = pick(odd, x_refs[3][r, :16, :], x_refs[1][r, :16, :])
    return before * lower, after * upper


def fill_ends(xp, x_refs, sides):
    batch, rows = x_refs[0].shape[:2]
    for r in range(batch):
        if sides is not None:
            before, after = row_ends(x_refs, r, sides)
        for c in range(D // 128):
            cols = slice(c * 128, (c + 1) * 128)
            zero = jnp.zeros((8, 128), F32)
            xp[r, c, 0:8, :] = zero if sides is None else before[8:, cols]
            xp[r, c, 8 + rows : 16 + rows, :] = zero if sides is None else after[:8, cols]
            xp[r, c, 8 : 8 + rows, :] = x_refs[0][r, :, cols].astype(F32)


def as_row(ref):
    return ref[...].astype(F32).reshape(1, ref.shape[0])


class Gather:
    def __init__(self, own, outs, send_sem, recv_sem):
        self.own, self.outs, self.send_sem, self.recv_sem = own, outs, send_sem, recv_sem
        dp, blk = lax.axis_index("dp"), lax.axis_index("blk")
        core, x = lax.rem(blk, 2), blk // 2
        self.core_peer = (dp, blk + 1 - 2 * core)
        self.x_peer = (dp, blk + 2 - 4 * x)

    def copy(self, i):
        source = self.outs[1] if i == 2 else self.own
        return pltpu.make_async_remote_copy(
            src_ref=source,
            dst_ref=self.outs[i],
            send_sem=self.send_sem.at[i],
            recv_sem=self.recv_sem.at[i],
            device_id=self.x_peer if i == 1 else self.core_peer,
            device_id_type=pl.DeviceIdType.MESH,
        )

    def begin(self):
        barrier = pltpu.get_barrier_semaphore()
        for device in (self.core_peer, self.x_peer):
            pl.semaphore_signal(
                barrier, inc=1, device_id=device, device_id_type=pl.DeviceIdType.MESH
            )
        pl.semaphore_wait(barrier, 2)
        self.copy(1).start()
        self.copy(0).start()

    def forward(self):
        self.copy(1).wait_recv()
        self.copy(2).start()

    def end(self):
        for i in (0, 2):
            self.copy(i).wait_recv()
        for i in range(3):
            self.copy(i).wait_send()


def pre_body(n_x, *refs):
    gather = None
    if n_x == 1:
        own, *refs = refs
        gather = Gather(own, refs[22:25], *refs[-2:])
        refs = refs[:22] + refs[25:-2]
    x_refs, refs = refs[:n_x], refs[n_x:]
    bias_query, bias_value, bias_point, bias_span, bias_unfold, depth_kernel = refs[:6]
    w_project, w_point, w_span, w_unfold, spread, perm = refs[6:12]
    q_out, k_out, v_out, p_out, kc_out, ker_out, dl_out, up_out, mix_out = refs[12:21]
    xp, vec = refs[21:]

    @pl.when(pl.program_id(0) == 0)
    def _():
        vec[16:24, :] = jnp.zeros((8, D), F32)
        vec[0:1, :ALL] = as_row(bias_query)
        vec[0:1, ALL:] = as_row(bias_value)
        vec[1:2, :ALL] = as_row(bias_point)
        vec[1:2, ALL:] = as_row(bias_unfold)
        vec[21:22, :TAPS] = as_row(bias_span)
        vec[8:17, :] = depth_kernel[...].astype(F32)
        if gather:
            gather.begin()

    batch, rows = x_refs[0].shape[:2]
    total_rows = batch * rows
    is_long = n_x > 1
    sides = row_sides() if is_long else None
    x = x_refs[0][...].reshape(total_rows, D)
    fill_ends(xp, x_refs, sides)
    bias_query = vec[0:1, :ALL]
    bias_value = vec[0:1, ALL:]
    by_row = lambda v: v.reshape(batch, rows, v.shape[-1])
    if is_long:
        q = (nn(x, w_project[:, :ALL]) + bias_query).astype(BF)
        for i in range(n_x):
            both = nn(x_refs[i][...].reshape(total_rows, D), w_project[:, ALL:])
            k_out[:, i * rows : (i + 1) * rows, :] = by_row(both[:, :ALL].astype(BF))
            v_out[:, i * rows : (i + 1) * rows, :] = by_row((both[:, ALL:] + bias_value).astype(BF))
    else:
        both = nn(x, w_project[...])
        q = (both[:, :ALL] + bias_query).astype(BF)
        k_out[...] = by_row(both[:, ALL : 2 * ALL].astype(BF))
        v_out[...] = by_row((both[:, 2 * ALL :] + bias_value).astype(BF))
    q_out[...] = by_row(q)

    for r in range(batch):
        for c in range(D // 128):
            cols = slice(c * 128, (c + 1) * 128)
            total = vec[8:9, cols] * xp[r, c, 4 : 4 + rows, :]
            for j in range(1, KERNEL):
                total += vec[8 + j : 9 + j, cols] * xp[r, c, 4 + j : 4 + j + rows, :]
            dl_out[r, :, cols] = total.astype(BF)
    key_conv = nn(dl_out[...].reshape(total_rows, D), w_point[...]) + vec[1:2, :ALL]
    kc_out[...] = by_row(key_conv)
    span = (key_conv * q.astype(F32)).astype(BF)
    span_weights = tn(w_span[...], perm[:TAPS, :]).astype(BF)
    span_bias = nn(vec[16:24, :128].astype(BF), perm[...])[5:6]
    logits = nn(span, span_weights) + span_bias
    lane = lax.broadcasted_iota(jnp.int32, (1, 128), 1)
    raised = jnp.where(lane < TAPS, jnp.exp(logits - window(logits, jnp.maximum)), 0.0)
    kernel = jnp.where(lane < TAPS, raised / window_sum(raised), 0.0)
    ker_out[...] = by_row(kernel)

    bias_unfold = vec[1:2, ALL:]
    unfold_rows = nn(x, w_unfold[...]) + bias_unfold
    for r in range(batch):
        if is_long:
            lower, upper, _ = sides
            ends = jnp.concatenate(row_ends(x_refs, r, sides), axis=0).astype(BF)
            unfold_ends = nn(ends, w_unfold[...]) + bias_unfold
        for c in range(PAIRS):
            cols = slice(c * 128, (c + 1) * 128)
            up_out[r, c, 8 : 8 + rows, :] = unfold_rows[r * rows : (r + 1) * rows, cols]
            if is_long:
                up_out[r, c, 0:8, :] = unfold_ends[8:16, cols] * lower
                up_out[r, c, 8 + rows : 16 + rows, :] = unfold_ends[16:24, cols] * upper
            else:
                zero = jnp.zeros((8, 128), F32)
                up_out[r, c, 0:8, :] = zero
                up_out[r, c, 8 + rows : 16 + rows, :] = zero

    if gather:

        @pl.when(pl.program_id(0) == pl.num_programs(0) - 1)
        def _():
            gather.forward()

    low_half = lane < HEAD
    parts = two_parts(kernel)
    scaled = q * jnp.asarray(HEAD ** (-0.5), BF)
    keys = k_out.shape[1]
    for p in range(PAIRS):
        cols = slice(p * 128, (p + 1) * 128)
        wide = nn(parts, spread[:, p * KERNEL * 128 : (p + 1) * KERNEL * 128])
        for r in range(batch):
            here = slice(r * rows, (r + 1) * rows)
            total = wide[here, :128] * up_out[r, p, 4 : 4 + rows, :]
            for j in range(1, KERNEL):
                total += wide[here, j * 128 : (j + 1) * 128] * up_out[r, p, 4 + j : 4 + j + rows, :]
            mix_out[r, :, ALL + p * 128 : ALL + (p + 1) * 128] = total.astype(BF)

            scores = nt(head_stack(k_out[r, :, cols], low_half), scaled[here, cols])
            for half in range(2):
                part = scores[half * keys : (half + 1) * keys]
                top = jnp.max(part, axis=0, keepdims=True)
                grown = jnp.exp(part - top)
                share = 1.0 / jnp.sum(grown, axis=0, keepdims=True)
                p_out[r, p, half * keys : (half + 1) * keys, :] = (grown * share).astype(BF)
            context = tn(head_stack(v_out[r, :, cols], low_half), p_out[r, p])
            mix_out[r, :, cols] = context.astype(BF).T

    if gather:

        @pl.when(pl.program_id(0) == pl.num_programs(0) - 1)
        def _():
            gather.end()


def fixed(array):
    zeros = (0,) * array.ndim
    return pl.BlockSpec(array.shape, lambda *_: zeros, pipeline_mode=pl.Buffered(1))


def per_row(*shape, batch=1):
    zeros = (0,) * len(shape)
    return pl.BlockSpec((batch, *shape), lambda i: (i, *zeros))


def in_vmem(shape, dtype):
    return pltpu.VMEM(shape, dtype)


def held(*arrays):
    return [pltpu.with_memory_space_constraint(a, pltpu.VMEM) for a in arrays]


def fetched(*arrays):
    return [pltpu.with_memory_space_constraint(a, pltpu.HBM) for a in arrays]


def params(name, **more):
    return pltpu.CompilerParams(vmem_limit_bytes=VMEM[name] * 1024 * 1024, **more)


def pre_call(xs, consts, batch, gathered=()):
    anywhere = pl.BlockSpec(memory_space=pl.ANY)
    count, rows = xs[0].shape[0], xs[0].shape[1]
    keys = rows * len(xs)
    shapes = [
        ((rows, ALL), BF),
        ((keys, ALL), BF),
        ((keys, ALL), BF),
        ((PAIRS, 2 * keys, rows), BF),
        ((rows, ALL), F32),
        ((rows, 128), F32),
        ((rows, D), BF),
        ((PAIRS, rows + 16, 128), F32),
        ((rows, D), BF),
    ]
    return pl.pallas_call(
        functools.partial(pre_body, len(xs)),
        grid=(count // batch,),
        in_specs=[anywhere] * len(gathered)
        + [per_row(rows, D, batch=batch)] * len(xs) + [fixed(c) for c in consts],
        out_specs=[per_row(*s, batch=batch) for s, _ in shapes] + [anywhere] * (3 * len(gathered)),
        out_shape=[
            (in_vmem if not gathered or i == 8 else pltpu.HBM)((count, *s), t)
            for i, (s, t) in enumerate(shapes)
        ]
        + [pltpu.HBM(g.shape, g.dtype) for g in gathered] * 3,
        scratch_shapes=[pltpu.VMEM((batch, D // 128, rows + 16, 128), F32), pltpu.VMEM((24, D), F32)]
        + [pltpu.SemaphoreType.DMA((3,))] * (2 * len(gathered)),
        compiler_params=params("pre_short", collective_id=1, has_side_effects=True)
        if gathered
        else params("pre_long"),
        cost_estimate=pl.CostEstimate(
            flops=count * rows * 6_000_000, bytes_accessed=20_000_000, transcendentals=1_000_000
        ),
        name="pre_long" if len(xs) > 1 else "pre_short",
    )(*fetched(*gathered, *xs, *consts))


def norm_stats(z):
    centre = z - jnp.mean(z, axis=-1, keepdims=True)
    inverse = lax.rsqrt(jnp.mean(centre * centre, axis=-1, keepdims=True) + 1e-12)
    return centre * inverse, inverse


def norm_back(upstream, normed, inverse, gain):
    scaled = upstream * gain
    plain = jnp.mean(scaled, axis=-1, keepdims=True)
    cross = jnp.mean(scaled * normed, axis=-1, keepdims=True)
    return inverse * (scaled - plain - normed * cross)


def fold8(values):
    return jnp.sum(values.reshape(values.shape[0] // 8, 8, values.shape[1]), axis=0)


def gelu_pair(v):
    cdf = 0.5 * (1.0 + lax.erf(v * ROOT_HALF))
    return v * cdf, cdf + v * jnp.exp(-0.5 * (v * v)) * DENSITY


def ffn_body(slot_rows, *refs):
    masked = slot_rows > 0
    if masked:
        live_ref, *refs = refs
    mix_ref, x_ref, cot_ref = refs[:3]
    vectors, (w_output, w_inner, w_outer) = refs[3:10], refs[10:13]
    out_ref, fig_ref, mg_ref, left, right, stat, slope, vec = refs[-8:]
    inl_ref, act_ref = right.at[:, :FF], right.at[:, FF : 2 * FF]
    step = pl.program_id(0)
    rows = x_ref.shape[1]

    @pl.when(step == 0)
    def _():
        stat[...] = jnp.zeros_like(stat)
        for i, ref in enumerate(vectors[:-1]):
            vec[2 + i : 3 + i, :] = as_row(ref)
        inner_row = as_row(vectors[-1])
        for i in range(FF // D):
            vec[8 + i : 9 + i, :] = inner_row[:, i * D : (i + 1) * D]

    x = x_ref[0]
    mixed = mix_ref[0]
    left[2 * D : 3 * D, :] = mixed.T
    left[3 * D :, :] = x.T
    first_normed, first_inverse = norm_stats(nn(mixed, w_output[...]) + vec[2:3, :] + x.astype(F32))
    first_norm = first_normed * vec[3:4, :] + vec[4:5, :]
    first_low = first_norm.astype(BF)
    left[:D, :] = first_low.T
    outer = []
    for g in range(GROUPS):
        for c in range(2):
            k = g * 2 + c
            inner = nn(first_low[:, g * ALL : (g + 1) * ALL], w_inner[g, :, c * D : (c + 1) * D])
            for r in range(0, rows, 16):
                act, slo = gelu_pair(inner[r : r + 16] + vec[8 + k : 9 + k, :])
                act_ref[r : r + 16, k * D : (k + 1) * D] = act.astype(BF)
                slope[r : r + 16, k * D : (k + 1) * D] = slo
        outer.append(nn(act_ref[:, g * 2 * D : (g + 1) * 2 * D], w_outer[g]))
    second_normed, second_inverse = norm_stats(
        jnp.concatenate(outer, axis=1) + vec[5:6, :] + first_norm
    )
    gain_second = vec[6:7, :]
    out_ref[0] = (second_normed * gain_second + vec[7:8, :]).astype(BF)
    seed = cot_ref[0].astype(F32)
    if masked:
        token = step * rows + lax.broadcasted_iota(jnp.int32, (rows, 1), 0)
        seed = jnp.where(token < live_ref[0, 0] * slot_rows, seed, 0.0)
    stat[0:8, :] += fold8(seed * second_normed)
    stat[8:16, :] += fold8(seed)
    second_grad = norm_back(seed, second_normed, second_inverse, gain_second)
    outer_low = second_grad.astype(BF)
    left[D : 2 * D, :] = outer_low.T
    stat[32:40, :] += fold8(outer_low.astype(F32))
    first_grad = []
    for g in range(GROUPS):
        for c in range(2):
            k = g * 2 + c
            back = nt(outer_low[:, g * ALL : (g + 1) * ALL], w_outer[g, c * D : (c + 1) * D, :])
            inl_ref[:, k * D : (k + 1) * D] = (back * slope[:, k * D : (k + 1) * D]).astype(BF)
        first_grad.append(nt(inl_ref[:, g * 2 * D : (g + 1) * 2 * D], w_inner[g]))
    first_grad = second_grad + jnp.concatenate(first_grad, axis=1)
    stat[16:24, :] += fold8(first_grad * first_normed)
    stat[24:32, :] += fold8(first_grad)
    first_in_grad = norm_back(first_grad, first_normed, first_inverse, vec[3:4, :])
    fig_ref[0] = first_in_grad
    attended_low = first_in_grad.astype(BF)
    right[:, 2 * FF :] = attended_low
    mg_ref[0] = nt(attended_low, w_output[...]).astype(BF)


def ffn_call(live, slot_rows, mixed, x, cotan, consts, joint, tokens):
    count, rows = x.shape[0], x.shape[1]
    total = count * rows
    masked = live is not None
    first = 0 if masked else (tokens - total) // rows
    n_in = (4 if masked else 3) + len(consts)
    out_shapes = [
        ((count, rows, D), BF, per_row(rows, D)),
        ((count, rows, D), F32, per_row(rows, D)),
        ((count, rows, D), BF, per_row(rows, D)),
        ((4 * D, tokens), BF, pl.BlockSpec((4 * D, rows), lambda i: (0, first + i))),
        ((tokens, 2 * FF + D), BF, pl.BlockSpec((rows, 2 * FF + D), lambda i: (first + i, 0))),
        ((40, D), F32, pl.BlockSpec((40, D), lambda i: (0, 0))),
    ]
    head = [live] if masked else []
    head_specs = [pl.BlockSpec(memory_space=pltpu.SMEM)] if masked else []
    return pl.pallas_call(
        functools.partial(ffn_body, slot_rows if masked else 0),
        grid=(count,),
        in_specs=head_specs
        + [per_row(rows, D)] * 3
        + [fixed(c) for c in consts]
        + [pl.BlockSpec(memory_space=pl.ANY)] * len(joint),
        out_specs=[s for _, _, s in out_shapes],
        out_shape=[
            (in_vmem if i in (1, 2) else pltpu.HBM)(s, t)
            for i, (s, t, _) in enumerate(out_shapes)
        ],
        scratch_shapes=[pltpu.VMEM((rows, FF), F32), pltpu.VMEM((16, D), F32)],
        input_output_aliases={n_in: 3, n_in + 1: 4} if masked else {},
        compiler_params=params("ffn_short" if masked else "ffn_long"),
        cost_estimate=pl.CostEstimate(
            flops=total * 12_000_000, bytes_accessed=30_000_000, transcendentals=total * FF
        ),
        name="ffn_short" if masked else "ffn_long",
    )(*head, *held(mixed), *fetched(x, cotan, *consts, *joint))


def post_body(n_x, *refs):
    is_long = n_x > 1
    x_refs = refs[:n_x]
    refs = refs[n_x:]
    (mg_ref, fig_ref, q_ref, k_ref, v_ref, p_ref, kc_ref, ker_ref, dl_ref, up_ref) = refs[:10]
    (depth_kernel, w_point, w_span, spread, perm) = refs[10:15]
    refs = refs[15:]
    if not is_long:
        (w_project, w_unfold), refs = refs[:2], refs[4:]
    (left, right, dkg), refs = refs[:3], refs[3:]
    if is_long:
        own_out, *far_outs = refs[:n_x]
        qt_out, ug_out, tg_out = refs[n_x : n_x + 3]
        xp, dgp, prp, dq_scr = refs[n_x + 3 :]
    else:
        tg_out, ru_out, dgp, prp, dq_scr = refs
    step = pl.program_id(0)
    batch, rows = x_refs[0].shape[:2]
    total_rows = batch * rows
    keys = k_ref.shape[1]
    ext = 8 if is_long else 0
    flat = lambda ref: ref[...].reshape(total_rows, ref.shape[-1])

    @pl.when(step == 0)
    def _():
        dkg[...] = jnp.zeros_like(dkg)
        dgp[...] = jnp.zeros_like(dgp)
        prp[...] = jnp.zeros_like(prp)

    if is_long:
        sides = lower, upper, odd = row_sides()
        fill_ends(xp, x_refs, sides)

        def send_rims(r, place, cols, total):
            before, after = total[:ext] * lower, total[ext + rows :] * upper
            far_outs[0][r, place : place + 8, cols] = pick(odd, before, after).astype(BF)
            far_outs[2][r, place : place + 8, cols] = pick(odd, after, before).astype(BF)


    q = flat(q_ref)
    qf = q.astype(F32)
    scaled = q * jnp.asarray(HEAD ** (-0.5), BF)
    low_half = lax.broadcasted_iota(jnp.int32, (1, 128), 1) < HEAD
    for p in range(PAIRS):
        cols = slice(p * 128, (p + 1) * 128)
        for r in range(batch):
            here = slice(r * rows, (r + 1) * rows)
            grad = mg_ref[r, :, cols]
            weight_grad = nt(head_stack(v_ref[r, :, cols], low_half), grad)
            low = []
            for half in range(2):
                part = slice(half * keys, (half + 1) * keys)
                probs = p_ref[r, p, part, :].astype(F32)
                inner = jnp.sum(probs * weight_grad[part], axis=0, keepdims=True)
                low.append((probs * (weight_grad[part] - inner)).astype(BF))
            score_low = jnp.concatenate(low, axis=0)
            value_grad = nn(p_ref[r, p], grad)
            value_grad = jnp.where(low_half, value_grad[:keys], value_grad[keys:])
            key_grad = nn(score_low, scaled[here, cols])
            key_grad = jnp.where(low_half, key_grad[:keys], key_grad[keys:])
            query_grad = tn(head_stack(k_ref[r, :, cols], low_half), score_low) * HEAD ** (-0.5)
            dq_scr[here, cols] = query_grad.T
            v_cols = slice(ALL + p * 128, ALL + (p + 1) * 128)
            if is_long:
                own_out[r, :, cols] = key_grad[:rows]
                own_out[r, :, v_cols] = value_grad[:rows]
                for i in range(1, n_x):
                    block = slice(i * rows, (i + 1) * rows)
                    far_outs[i - 1][r, :rows, cols] = key_grad[block].astype(BF)
                    far_outs[i - 1][r, :rows, v_cols] = value_grad[block].astype(BF)
            else:
                ru_out[here, 2 * ALL + p * 128 : 2 * ALL + (p + 1) * 128] = key_grad.astype(BF)
                ru_out[here, 3 * ALL + p * 128 : 3 * ALL + (p + 1) * 128] = value_grad.astype(BF)

    kernel = flat(ker_ref)
    parts = two_parts(kernel)
    kernel_grad = jnp.zeros((total_rows, 128), F32)
    span_rows = rows + 2 * ext
    for p in range(PAIRS):
        cols = slice(p * 128, (p + 1) * 128)
        table = slice(p * KERNEL * 128, (p + 1) * KERNEL * 128)
        wide = nn(parts, spread[:, table])
        all_products = []
        for r in range(batch):
            here = slice(r * rows, (r + 1) * rows)
            grad = mg_ref[r, :, ALL + p * 128 : ALL + (p + 1) * 128].astype(F32)
            products = []
            for j in range(KERNEL):
                products.append((grad * up_ref[r, p, 4 + j : 4 + j + rows, :]).astype(BF))
                prp[r, j, 16 : 16 + rows, :] = wide[here, j * 128 : (j + 1) * 128] * grad
            all_products.append(jnp.concatenate(products, axis=1))
            first = 20 - ext
            total = prp[r, 0, first : first + span_rows, :]
            for j in range(1, KERNEL):
                total += prp[r, j, first - j : first - j + span_rows, :]
            if is_long:
                ug_out[r, :, cols] = total[ext : ext + rows]
                send_rims(r, rows + 8, cols, total)
            else:
                ru_out[here, cols] = total.astype(BF)
        kernel_grad += nt(jnp.concatenate(all_products, axis=0), spread[:128, table])
    if is_long:
        zero = jnp.zeros((batch, 8, ALL), BF)
        far_outs[0][:, rows + 8 : rows + 16, ALL:] = zero
        far_outs[-1][:, rows + 8 : rows + 16, ALL:] = zero

    logit_low = (kernel * (kernel_grad - window_sum(kernel * kernel_grad))).astype(BF)
    left[D:, :] = nt(perm[...], logit_low).astype(BF)
    span_grad = nn(logit_low, tn(perm[:TAPS, :], w_span[...]).astype(BF))
    key_conv = flat(kc_ref)
    right[:, ALL:] = (key_conv * qf).astype(BF)
    left[:D, :] = flat(dl_ref).T
    point_low = (span_grad * qf).astype(BF)
    right[:, :ALL] = point_low
    query_total = (dq_scr[...] + span_grad * key_conv).astype(BF)
    depth_grad = nt(point_low, w_point[...])
    for r in range(batch):
        for c in range(D // 128):
            dgp[r, c, 16 : 16 + rows, :] = depth_grad[
                r * rows : (r + 1) * rows, c * 128 : (c + 1) * 128
            ]

    if not is_long:
        ru_out[:, ALL : 2 * ALL] = query_total
        base = nt(ru_out[:, :ALL], w_unfold[...]) + nt(ru_out[:, ALL:], w_project[...])
    else:
        qt_out[...] = query_total.reshape(batch, rows, ALL)
    for c in range(D // 128):
        cols = slice(c * 128, (c + 1) * 128)
        for r in range(batch):
            x_part = xp[r, c] if is_long else x_refs[0][r, :, cols].astype(F32)
            first = 20 - ext
            total = None
            for j in range(KERNEL):
                moved = dgp[r, c, first - j : first - j + span_rows, :]
                term = depth_kernel[j : j + 1, cols].astype(F32) * moved
                total = term if total is None else total + term
                dkg[j * 8 : (j + 1) * 8, cols] += fold8(moved * x_part)
            if is_long:
                tg_out[r, :, cols] = total[ext : ext + rows] + fig_ref[r, :, cols]
                send_rims(r, rows, cols, total)
            else:
                tg_out[r, :, cols] = total + fig_ref[r, :, cols] + base[r * rows : (r + 1) * rows, cols]


def post_call(xs, mg, fig, kept, consts, joint, tokens, batch):
    count, rows = xs[0].shape[0], xs[0].shape[1]
    keys = rows * len(xs)
    total = count * rows
    is_long = len(xs) > 1
    wide = batch * rows
    first = (tokens - total) // wide if is_long else 0
    row_args = [mg, fig, *kept]
    outs = [
        ((D + 128, tokens), BF, pl.BlockSpec((D + 128, wide), lambda i: (0, first + i))),
        ((tokens, 2 * ALL), BF, pl.BlockSpec((wide, 2 * ALL), lambda i: (first + i, 0))),
        ((KERNEL * 8, D), F32, pl.BlockSpec((KERNEL * 8, D), lambda i: (0, 0))),
    ]
    row_out = lambda r, c, t: ((count, r, c), t, per_row(r, c, batch=batch))
    scratch = []
    if is_long:
        outs.append(row_out(rows, D, F32))
        for i in range(1, len(xs)):
            outs.append(row_out(rows + 16 if i in (1, len(xs) - 1) else rows, D, BF))
        outs += [row_out(rows, ALL, BF), row_out(rows, ALL, F32), row_out(rows, D, F32)]
        scratch.append(pltpu.VMEM((batch, D // 128, rows + 16, 128), F32))
    else:
        outs += [
            row_out(rows, D, F32),
            ((tokens, 4 * ALL), BF, pl.BlockSpec((wide, 4 * ALL), lambda i: (first + i, 0))),
        ]
    scratch += [
        pltpu.VMEM((batch, D // 128, rows + 32, 128), F32),
        pltpu.VMEM((batch, KERNEL, rows + 32, 128), F32),
        pltpu.VMEM((wide, ALL), F32),
    ]
    row_args = held(*row_args) if is_long else held(mg, fig) + fetched(*row_args[2:])
    inputs = [*fetched(*xs), *row_args, *fetched(*consts)]
    return pl.pallas_call(
        functools.partial(post_body, len(xs)),
        grid=(count // batch,),
        in_specs=[per_row(rows, D, batch=batch)] * len(xs)
        + [per_row(*a.shape[1:], batch=batch) for a in row_args]
        + [fixed(c) for c in consts]
        + [pl.BlockSpec(memory_space=pl.ANY)] * len(joint),
        out_specs=[s for _, _, s in outs],
        out_shape=[
            (in_vmem if is_long and i in (3, 7, 8, 9) else pltpu.HBM)(s, t)
            for i, (s, t, _) in enumerate(outs)
        ],
        scratch_shapes=scratch,
        input_output_aliases={len(inputs) + i: i for i in range(len(joint))},
        compiler_params=params("post_long" if is_long else "post_short"),
        cost_estimate=pl.CostEstimate(
            flops=total * 10_000_000, bytes_accessed=30_000_000, transcendentals=0
        ),
        name="post_long" if is_long else "post_short",
    )(*inputs, *fetched(*joint))


def end_body(n_x, *refs):
    own, *rest = refs[:n_x]
    qt, ug, tg, w_project, w_unfold, _, out_ref, ru_out = refs[n_x:]
    rows = own.shape[1]
    both = own[0]
    for far in rest:
        both = both + far[0, :rows, :].astype(F32)
    _, _, odd = row_sides()
    unfold = ug[0]
    after = pick(odd, rest[2][0, rows:, :], rest[0][0, rows:, :])
    before = pick(odd, rest[0][0, rows:, :], rest[2][0, rows:, :])
    middle = unfold[8 : rows - 8]
    ru_out[:, :ALL] = jnp.concatenate(
        [unfold[:8] + before[8:, :ALL], middle, unfold[rows - 8 :] + after[8:, :ALL]], axis=0
    ).astype(BF)
    ru_out[:, ALL : 2 * ALL] = qt[0]
    ru_out[:, 2 * ALL :] = both.astype(BF)
    total = nt(ru_out[:, :ALL], w_unfold[...]) + nt(ru_out[:, ALL:], w_project[...]) + tg[0]
    out_ref[0] = total
    out_ref[0, :8, :] = total[:8] + before[:8]
    out_ref[0, rows - 8 :, :] = total[rows - 8 :] + after[:8]


def end_call(own, far, qt, ug, tg, w_project, w_unfold, joint):
    count, rows = own.shape[0], own.shape[1]
    first = (joint.shape[0] - count * rows) // rows
    (own,), (qt, ug, tg) = held(own), held(qt, ug, tg)
    row_args = [own, *fetched(*far), qt, ug, tg]
    return pl.pallas_call(
        functools.partial(end_body, 1 + len(far)),
        grid=(count,),
        in_specs=[per_row(*a.shape[1:]) for a in row_args]
        + [fixed(w_project), fixed(w_unfold), pl.BlockSpec(memory_space=pl.ANY)],
        out_specs=[per_row(rows, D), pl.BlockSpec((rows, 4 * ALL), lambda i: (first + i, 0))],
        out_shape=[
            jax.ShapeDtypeStruct((count, rows, D), F32),
            jax.ShapeDtypeStruct(joint.shape, BF),
        ],
        input_output_aliases={len(row_args) + 2: 1},
        compiler_params=params("end"),
        cost_estimate=pl.CostEstimate(
            flops=count * rows * 2_400_000, bytes_accessed=10_000_000, transcendentals=0
        ),
        name="end_long",
    )(*row_args, *fetched(w_project, w_unfold, joint))


UNIT = 3 * ALL
CHUNK = 4 * UNIT
CHUNKS = 8
LAST = 6 * 512
PACKED = (CHUNKS - 1) * CHUNK + LAST
SPAN_ROW = (CHUNKS - 1) * CHUNK + 2 * UNIT
SMALL_ROW = SPAN_ROW + ALL
SMALL = 48
MESH = pl.DeviceIdType.MESH


CHUNK_PARTS = (
    ((0, 2560, "cxyz"), (2560, 2048, "cyxz")),
    ((4608, 2560, "cxyz"), (7168, 2048, "cyxz")),
    ((9216, 2560, "cxyz"), (11776, 2048, "cyxz")),
    ((13824, 1536, "cxyz"), (15360, 3072, "cyxz")),
    ((18432, 2048, "cyxz"), (20480, 2048, "cxyz"), (22528, 512, "czxy")),
    ((23040, 2048, "cxyz"), (25088, 1024, "czxy"), (26112, 1536, "cyxz")),
    ((27648, 1536, "cxyz"), (29184, 1024, "czyx"), (30208, 2048, "cyxz")),
    ((32256, 1024, "cyxz"), (33280, 1536, "cxyz"), (34816, 512, "cyzx")),
)
PARTS = sum(CHUNK_PARTS, ())


def rows_of(ref, start, count):
    return ref.at[pl.ds(pl.multiple_of(start, 16), count), :]


def add_rows(out, start, sources, count):
    step = next(s for s in (160, 128, 96, 80, 64, 48, 32, 16) if count % s == 0)

    def body(i, carry):
        total = None
        for ref, first in sources:
            value = rows_of(ref, first + i * step, step)[...].astype(F32)
            total = value if total is None else total + value
        rows_of(out, start + i * step, step)[...] = total.astype(BF)
        return carry

    lax.fori_loop(0, count // step, body, 0)


class Exchange:
    def __init__(self, source, res, out, got, sems):
        self.source, self.res, self.out, self.got = source, res, out, got
        self.send_sem, self.recv_sem, self.out_sem = sems
        dp, blk = lax.axis_index("dp"), lax.axis_index("blk")
        core, x, y, z = lax.rem(blk, 2), blk // 2, lax.rem(dp, 2), dp // 2
        self.index = {"c": core, "x": x, "y": y, "z": z}
        self.peers = {
            "c": [(dp, blk + 1 - 2 * core)],
            "x": [(dp, blk + 2 - 4 * x)],
            "y": [(dp + 1 - 2 * y, blk)],
            "z": [(lax.rem(z + i, 4) * 2 + y, blk) for i in (1, 2, 3)],
        }
        self.sizes, self.slots, self.places = [], [], []
        used = 0
        for _, count, order in PARTS:
            sizes, slots, places = [count], [0], []
            for axis in order:
                sizes.append(sizes[-1] // (len(self.peers[axis]) + 1))
                slots.append(slots[-1] + len(self.peers[axis]))
                places.append(used)
                used += sizes[-1] * len(self.peers[axis])
            self.sizes.append(sizes)
            self.slots.append(slots)
            self.places.append(places)

    def greet(self):
        barrier = pltpu.get_barrier_semaphore()
        for devices in self.peers.values():
            for device in devices:
                pl.semaphore_signal(barrier, inc=1, device_id=device, device_id_type=MESH)

    def await_greetings(self):
        pl.semaphore_wait(pltpu.get_barrier_semaphore(), 6)

    def sum_at(self, n, level):
        return (self.source, PARTS[n][0]) if level == 0 else (self.got, self.places[n][level - 1])

    def held(self, n, level):
        row, _, order = PARTS[n]
        for i in range(level):
            row = row + self.index[order[i]] * self.sizes[n][i + 1]
        return row

    def copies(self, n, level, back):
        axis = PARTS[n][2][level]
        size = self.sizes[n][level + 1]
        result = []
        for i, device in enumerate(self.peers[axis]):
            if back:
                source = target = rows_of(self.res, self.held(n, level + 1), size)
            else:
                ref, first = self.sum_at(n, level)
                theirs = lax.rem(self.index[axis] + i + 1, len(self.peers[axis]) + 1)
                source = rows_of(ref, first + theirs * size, size)
                target = rows_of(self.got, self.places[n][level] + i * size, size)
            slot = self.slots[n][level] + i + (6 if back else 0)
            result.append(
                pltpu.make_async_remote_copy(
                    src_ref=source,
                    dst_ref=target,
                    send_sem=self.send_sem.at[n, slot],
                    recv_sem=self.recv_sem.at[n, slot],
                    device_id=device,
                    device_id_type=MESH,
                )
            )
        return result

    def copy_out(self, n):
        row, count, _ = PARTS[n]
        return pltpu.make_async_copy(
            rows_of(self.res, row, count), rows_of(self.out, row, count), self.out_sem.at[n]
        )

    def stage(self, n, s):
        if s:
            for copy in self.copies(n, s - 1 if s <= 4 else 8 - s, s > 4):
                copy.wait_recv()
        if 1 <= s <= 4:
            level = s - 1
            axis = PARTS[n][2][level]
            size = self.sizes[n][s]
            ref, first = self.sum_at(n, level)
            terms = [(ref, first + self.index[axis] * size)]
            terms += [
                (self.got, self.places[n][level] + i * size) for i in range(len(self.peers[axis]))
            ]
            into, start = self.sum_at(n, s) if s < 4 else (self.res, self.held(n, 4))
            add_rows(into, start, terms, size)
        if s < 8:
            for copy in self.copies(n, s if s < 4 else 7 - s, s >= 4):
                copy.start()
        else:
            self.copy_out(n).start()

    def finish(self):
        for n in range(len(PARTS)):
            for level in range(4):
                for back in (False, True):
                    for copy in self.copies(n, level, back):
                        copy.wait_send()
            self.copy_out(n).wait()


def weights_body(remote, ranges, *refs):
    left, right, left_post, right_post, rows_grad, stat_a, stat_b, depth_a, depth_b, out = refs[:10]
    held_left, held_right, sums, part, load_sem = refs[10:15]
    scratch = refs[15:]
    tokens = held_left.shape[2]

    def loads(k):
        slot = k % 2
        if k < 4:
            a, a_rows, b, b_cols = left, (k * ALL, ALL), right, (k * 4 * ALL, 4 * ALL)
        elif k == 4:
            a, a_rows, b, b_cols = left, (2 * D, D), right, (2 * FF, D)
        elif k < 7:
            a, a_rows, b, b_cols = left, (3 * D + (k - 5) * ALL, ALL), rows_grad, (0, 4 * ALL)
        else:
            a, a_rows, b, b_cols = left_post, (0, D + 128), right_post, (0, D)
        copies = []
        for i, (to, start, size) in enumerate(ranges):
            here, there = pl.ds(to, size), pl.ds(start, size)
            copies.append(
                pltpu.make_async_copy(
                    a.at[pl.ds(*a_rows), there],
                    held_left.at[slot, : a_rows[1], here],
                    load_sem.at[slot, 2 * i],
                )
            )
            copies.append(
                pltpu.make_async_copy(
                    b.at[there, pl.ds(*b_cols)],
                    held_right.at[slot, here, : b_cols[1]],
                    load_sem.at[slot, 2 * i + 1],
                )
            )
        return copies

    def compute(k):
        for copy in loads(k):
            copy.wait()
        if k + 1 < CHUNKS:
            for copy in loads(k + 1):
                copy.start()
        slot = k % 2
        by_left = {4: 2, 7: 1}.get(k, 4)

        def unit(j, carry):
            if by_left == 4:
                a, b = 0, j
            elif by_left == 2:
                a, b = j // 2, lax.rem(j, 2)
            else:
                a, b = j, 0
            lhs = held_left[slot, pl.ds(pl.multiple_of(a * ALL, ALL), ALL), :]
            rhs = held_right[slot, :, pl.ds(pl.multiple_of(b * ALL, ALL), ALL)]
            value = nn(lhs, rhs)
            for c in range(3):
                rows_of(part, k * CHUNK + j * UNIT + c * ALL, ALL)[...] = value[
                    :, c * 128 : (c + 1) * 128
                ].astype(BF)
            return carry

        lax.fori_loop(0, 2 if k == 7 else 4, unit, 0)
        ones = jnp.ones((16, tokens), BF)
        if k in (0, 1, 4, 5):
            wide = 2 if k == 4 else 4
            first = {0: 28, 1: 32, 4: 36, 5: 38}[k]
            total = nn(ones, held_right[slot, :, : wide * ALL])
            for j in range(wide):
                sums[first + j : first + j + 1, :] = total[0:1, j * ALL : (j + 1) * ALL]
        if k == 7:
            span = nn(held_left[slot, D:, :], held_right[slot, :, ALL:D])
            for c in range(3):
                part[SPAN_ROW + c * 128 : SPAN_ROW + (c + 1) * 128, :] = span[
                    :, c * 128 : (c + 1) * 128
                ].astype(BF)
            sums[42:43, :] = nn(ones, held_right[slot, :, :ALL])[0:1]
            sums[43:44, :128] = nt(ones, held_left[slot, D:, :])[0:1]
            for first, a, b in ((0, stat_a, stat_b), (10, depth_a, depth_b)):
                for i in range(a.shape[0] // 8):
                    both = jnp.sum(a[i * 8 : i * 8 + 8] + b[i * 8 : i * 8 + 8], axis=0, keepdims=True)
                    sums[first + 2 * i : first + 2 * i + 1, :] = both[:, :ALL]
                    sums[first + 2 * i + 1 : first + 2 * i + 2, :] = both[:, ALL:]
            small = sums[...].astype(BF)
            for c in range(3):
                part[SMALL_ROW + c * SMALL : SMALL_ROW + (c + 1) * SMALL, :] = small[
                    :, c * 128 : (c + 1) * 128
                ]
            part[SMALL_ROW + 3 * SMALL :, :] = jnp.zeros((PACKED - SMALL_ROW - 3 * SMALL, 128), BF)

    for copy in loads(0):
        copy.start()
    sums[...] = jnp.zeros_like(sums)
    if not remote:
        for k in range(CHUNKS):
            compute(k)
        pltpu.sync_copy(part, out)
        return
    res, got, *sems = scratch
    exchange = Exchange(part, res, out, got, sems)
    exchange.greet()
    for t in range(CHUNKS + 8):
        if t < CHUNKS:
            compute(t)
        if t == 0:
            exchange.await_greetings()
        for k in reversed(range(CHUNKS)):
            if 0 <= t - k <= 8:
                first = sum(len(p) for p in CHUNK_PARTS[:k])
                for n in range(first, first + len(CHUNK_PARTS[k])):
                    exchange.stage(n, t - k)
    exchange.finish()


def weights_call(remote, n_short, n_long, big, small):
    tokens = n_short + n_long
    padded = big[1].shape[0]
    n_parts = len(PARTS)
    scratch = [
        pltpu.VMEM((2, D + 128, tokens), BF),
        pltpu.VMEM((2, tokens, 4 * ALL), BF),
        pltpu.VMEM((SMALL, ALL), F32),
        pltpu.VMEM((PACKED, 128), BF),
        pltpu.SemaphoreType.DMA((2, 4)),
    ]
    if remote:
        scratch += [
            pltpu.VMEM((PACKED, 128), BF),
            pltpu.VMEM((PACKED - PACKED // 32, 128), BF),
            pltpu.SemaphoreType.DMA((n_parts, 12)),
            pltpu.SemaphoreType.DMA((n_parts, 12)),
            pltpu.SemaphoreType.DMA((n_parts,)),
        ]
    more = dict(collective_id=0, has_side_effects=True) if remote else {}
    return pl.pallas_call(
        functools.partial(weights_body, remote, ((0, 0, n_short), (n_short, padded - n_long, n_long))),
        in_specs=[pl.BlockSpec(memory_space=pl.ANY)] * len(big)
        + [pl.BlockSpec(memory_space=pltpu.VMEM)] * len(small),
        out_specs=pl.BlockSpec(memory_space=pl.ANY),
        out_shape=pltpu.VMEM((PACKED, 128), BF) if remote else jax.ShapeDtypeStruct((PACKED, 128), BF),
        scratch_shapes=scratch,
        compiler_params=params("weights", **more),
        cost_estimate=pl.CostEstimate(
            flops=2 * 31 * ALL * ALL * tokens, bytes_accessed=50_000_000, transcendentals=0
        ),
        name="weights",
    )(*fetched(*big, *small))


SMALL_OUTS = [
    ("gain_second", 0, D),
    ("shift_second", 2, D),
    ("gain_first", 4, D),
    ("shift_first", 6, D),
    ("bias_outer", 8, D),
    ("bias_inner", 28, FF),
    ("bias_output", 36, D),
    ("bias_unfold", 38, ALL),
    ("bias_query", 39, ALL),
    ("bias_value", 41, ALL),
    ("bias_point", 42, ALL),
    ("bias_span", 43, TAPS),
]


def unpack_body(block, inner, outer, output, unfold, project, point, span, depth, *small):
    step = pl.program_id(0)

    def tile(unit):
        start = unit * UNIT
        return jnp.concatenate(
            [block[start + c * ALL : start + (c + 1) * ALL, :] for c in range(3)], axis=1
        )

    @pl.when(step < 2)
    def _():
        for i in range(4):
            inner[0, :, i * ALL : (i + 1) * ALL] = tile(i).astype(F32)

    @pl.when((step >= 2) & (step < 4))
    def _():
        for i in range(4):
            outer[0, i * ALL : (i + 1) * ALL, :] = tile(i).T.astype(F32)

    @pl.when(step == 4)
    def _():
        for i in range(4):
            a, b = divmod(i, 2)
            output[a * ALL : (a + 1) * ALL, b * ALL : (b + 1) * ALL] = tile(i).astype(F32)

    @pl.when((step == 5) | (step == 6))
    def _():
        unfold[...] = tile(0).astype(F32)
        for i in range(3):
            project[:, i * ALL : (i + 1) * ALL] = tile(i + 1).astype(F32)

    @pl.when(step == 7)
    def _():
        for i in range(2):
            point[i * ALL : (i + 1) * ALL, :] = tile(i).astype(F32)
        tail = 2 * UNIT
        wide = jnp.concatenate(
            [block[tail + c * 128 : tail + (c + 1) * 128, :] for c in range(3)], axis=1
        )
        span[...] = wide[:TAPS].astype(F32)
        tail += ALL
        rows = jnp.concatenate(
            [block[tail + c * SMALL : tail + (c + 1) * SMALL, :] for c in range(3)], axis=1
        ).astype(F32)
        for j in range(KERNEL):
            for half in range(2):
                place = 10 + 2 * j + half
                depth[j : j + 1, half * ALL : (half + 1) * ALL] = rows[place : place + 1]
        for ref, (_, first, size) in zip(small, SMALL_OUTS):
            for i in range(max(1, size // ALL)):
                wide = min(size, ALL)
                ref[i * ALL : i * ALL + wide] = rows[first + i, :wide]


def unpack_call(packed):
    def at(first, count):
        return lambda s: jnp.clip(s - first, 0, count - 1)

    inner_at, outer_at, rows_at = at(0, 2), at(2, 2), at(5, 2)
    whole = lambda *shape: (shape, pl.BlockSpec(shape, lambda s: (0,) * len(shape)))
    specs = [
        ((GROUPS, ALL, 4 * ALL), pl.BlockSpec((1, ALL, 4 * ALL), lambda s: (inner_at(s), 0, 0))),
        ((GROUPS, 4 * ALL, ALL), pl.BlockSpec((1, 4 * ALL, ALL), lambda s: (outer_at(s), 0, 0))),
        whole(D, D),
        ((D, ALL), pl.BlockSpec((ALL, ALL), lambda s: (rows_at(s), 0))),
        ((D, 3 * ALL), pl.BlockSpec((ALL, 3 * ALL), lambda s: (rows_at(s), 0))),
        whole(D, ALL),
        whole(TAPS, ALL),
        whole(KERNEL, D),
    ]
    specs += [whole(size) for _, _, size in SMALL_OUTS]
    return pl.pallas_call(
        unpack_body,
        grid=(CHUNKS,),
        in_specs=[pl.BlockSpec((CHUNK, 128), lambda s: (s, 0))],
        out_specs=[b for _, b in specs],
        out_shape=[jax.ShapeDtypeStruct(s, F32) for s, _ in specs],
        compiler_params=params("unpack"),
        cost_estimate=pl.CostEstimate(flops=0, bytes_accessed=27_000_000, transcendentals=0),
        name="unpack",
    )(packed)


def shards(
    long_input,
    short_input,
    long_cotan,
    short_cotan,
    live_slots,
    w_project,
    bias_query,
    bias_value,
    depth_kernel,
    w_point,
    bias_point,
    w_span,
    bias_span,
    w_unfold,
    bias_unfold,
    w_output,
    bias_output,
    gain_first,
    shift_first,
    w_inner,
    bias_inner,
    w_outer,
    bias_outer,
    gain_second,
    shift_second,
):
    n_blk = lax.axis_size("blk")
    short_x = short_input.reshape(short_input.shape[2:])
    short_cot = short_cotan.reshape(short_cotan.shape[2:])
    perm, spread = (jnp.asarray(t) for t in tap_tables())
    span_t = w_span.T
    pre_consts = (
        bias_query, bias_value, bias_point, bias_span, bias_unfold, depth_kernel,
        w_project, w_point, span_t, w_unfold, spread, perm,
    )
    ffn_consts = (
        bias_output, gain_first, shift_first, bias_outer, gain_second, shift_second, bias_inner,
        w_output, w_inner, w_outer,
    )
    *short_kept, short_mixed, near, far, both = pre_call(
        [short_x], pre_consts, SHORT_BATCH, (long_input,)
    )
    xs = [long_input, near, far, both]
    *long_kept, long_mixed = pre_call(xs, pre_consts, long_input.shape[0])

    n_long, n_short = (a.shape[0] * a.shape[1] for a in (long_input, short_x))
    tokens = (pl.cdiv(n_short, n_long) + 1) * n_long
    as_long = lambda a: a.reshape(-1, FFN_LONG, D)
    l_out, l_fig, l_mg, *joint, l_stat = ffn_call(
        None, 0, *map(as_long, (long_mixed, long_input, long_cotan)), ffn_consts, (), tokens
    )
    l_out, l_fig, l_mg = (a.reshape(long_input.shape) for a in (l_out, l_fig, l_mg))
    s_out, s_fig, s_mg, left, right, s_stat = ffn_call(
        live_slots,
        short_x.shape[1],
        *(a.reshape(-1, FFN_ROWS, D) for a in (short_mixed, short_x, short_cot)),
        ffn_consts,
        joint,
        tokens,
    )
    s_fig, s_mg = s_fig.reshape(short_x.shape), s_mg.reshape(short_x.shape)
    post_consts = (depth_kernel, w_point, span_t, spread, perm)
    l_post = post_call(xs, l_mg, l_fig, long_kept, post_consts, (), tokens, LONG_BATCH)
    (*joint, l_dkg, own), l_rest = l_post[:4], l_post[4:]
    far, (l_qt, l_ug, l_tg) = l_rest[: n_blk - 1], l_rest[n_blk - 1 :]
    far = [
        lax.ppermute(a, "blk", [(i, i ^ k) for i in range(n_blk)])
        for k, a in enumerate(far, 1)
    ]
    left_post, right_post, s_dkg, short_grad, rows_grad = post_call(
        [short_x], s_mg, s_fig, short_kept, post_consts + (w_project, w_unfold), joint, tokens, SHORT_BATCH
    )
    long_grad, rows_grad = end_call(own, far, l_qt, l_ug, l_tg, w_project, w_unfold, rows_grad)

    remote = lax.axis_size("dp") == 8 and n_blk == 4
    packed = weights_call(
        remote, n_short, n_long, (left, right, left_post, right_post, rows_grad), (l_stat, s_stat, l_dkg, s_dkg)
    )
    if not remote:
        packed = lax.psum(packed, ("dp", "blk"))
    if remote:
        packed = pltpu.with_memory_space_constraint(packed, pltpu.VMEM)
    inner, outer, output, unfold, project, point, span, depth, *small = unpack_call(packed)
    named = {name: value for (name, _, _), value in zip(SMALL_OUTS, small)}
    return (
        l_out,
        s_out.reshape(short_input.shape),
        long_grad,
        short_grad.reshape(short_input.shape),
        project,
        named["bias_query"],
        named["bias_value"],
        depth,
        point,
        named["bias_point"],
        span.T,
        named["bias_span"],
        unfold,
        named["bias_unfold"],
        output,
        named["bias_output"],
        named["gain_first"],
        named["shift_first"],
        inner,
        named["bias_inner"],
        outer,
        named["bias_outer"],
        named["gain_second"],
        named["shift_second"],
    )


def solution(mesh):
    rows = P("dp", "blk", None)
    slots = P("dp", "blk", None, None, None)
    in_specs = (rows, slots, rows, slots, P("dp", "blk")) + (P(),) * 20
    out_specs = (rows, slots, rows, slots) + (P(),) * 20
    return jax.shard_map(shards, mesh=mesh, in_specs=in_specs, out_specs=out_specs, check_vma=False)
```

profile of v0, /device:TPU:1, one launch (start us, length us, event | category | flops | bytes accessed | tf_op | source)
XLA Modules:
  0.0 233.1 jit_solution(6317577897053817260)
XLA Ops:
  0.7 23.5 %pre_short.1 = (bf16[8,128,384]{2,1,0:T(8,128)(2,1)}, bf16[8,128,384]{2,1,0:T(8,128)(2,1)}, bf16[8,128,384]{2,1,0:T(8,128)(2,1)}, bf16[8,3,256,128]{3,2,1,0:T(8,...) custom-call(bf16[3,128,768]{2,1,0:T(8,128)(2,1)} %refs_0_.6, ...), custom_call_target="tpu_custom_call" | custom-call | flops 6144000000 | bytes 20000000 | tf_op jit(solution)/shard_map/pre_short/pallas_call | solution.py:329
  24.1 11.8 %pre_long.1 = (bf16[3,128,384]{2,1,0:T(8,128)(2,1)S(1)}, bf16[3,512,384]{2,1,0:T(8,128)(2,1)S(1)}, bf16[3,512,384]{2,1,0:T(8,128)(2,1)S(1)}, bf16[3,3,1024,128]{...) custom-call(bf16[3,128,768]{2,1,0:T(8,128)(2,1)} %refs_0_.6, ...), custom_call_target="tpu_custom_call" | custom-call | flops 2304000000 | bytes 20000000 | tf_op jit(solution)/shard_map/pre_long/pallas_call | solution.py:329
  35.9 15.0 %ffn_long.1 = (bf16[1,384,768]{2,1,0:T(8,128)(2,1)}, f32[1,384,768]{2,1,0:T(8,128)S(1)}, bf16[1,384,768]{2,1,0:T(8,128)(2,1)S(1)}, bf16[3072,1536]{1,0:T(8,128)(...) custom-call(bf16[1,384,768]{2,1,0:T(8,128)(2,1)S(1)} %bitcast.21, bf16[1,384,768]{2,1,0:T(8,128)(2,1)} %bitcast.27, ...), custom_call_target="tpu_custom_call" | custom-call | flops 4608000000 | bytes 30000000 | tf_op jit(solution)/shard_map/ffn_long/pallas_call | solution.py:460
  51.0 13.5 %post_long.1 = (bf16[896,1536]{1,0:T(8,128)(2,1)}, bf16[1536,768]{1,0:T(8,128)(2,1)}, f32[72,768]{1,0:T(8,128)}, f32[3,128,768]{2,1,0:T(8,128)S(1)}, bf16[3,144,...) custom-call(bf16[3,128,768]{2,1,0:T(8,128)(2,1)} %refs_0_.6, ...), custom_call_target="tpu_custom_call" | custom-call | flops 3840000000 | bytes 30000000 | tf_op jit(solution)/shard_map/post_long/pallas_call | solution.py:660
  64.4 0.8 collective-permute-start.1
  65.3 0.4 collective-permute-start
  65.7 0.6 collective-permute-start.2
  67.0 30.2 %ffn_short.1 = (bf16[4,256,768]{2,1,0:T(8,128)(2,1)}, f32[4,256,768]{2,1,0:T(8,128)S(1)}, bf16[4,256,768]{2,1,0:T(8,128)(2,1)S(1)}, bf16[3072,1536]{1,0:T(8,128)...) custom-call(s32[1,1]{1,0:T(1,128)S(6)} %copy.61.refs_0_, ...), custom_call_target="tpu_custom_call", output_to_operand_aliasing={{3}: (14, {}), {4}: (15, {})} | custom-call | flops 12288000000 | bytes 30000000 | tf_op jit(solution)/shard_map/ffn_short/pallas_call | solution.py:460
  97.3 23.5 %post_short.1 = (bf16[896,1536]{1,0:T(8,128)(2,1)}, bf16[1536,768]{1,0:T(8,128)(2,1)}, f32[72,768]{1,0:T(8,128)}, f32[8,128,768]{2,1,0:T(8,128)}, bf16[1536,1536]{1,0:T(8,128)(2,1)}) custom-call(bf16[8,128,768]{2,1,0:T(8,128)(2,1)} %bitcast.25, bf16[8,128,768]{2,1,0:T(8,128)(2,1)S(1)} %bitcast.18, ...), custom_call_target="tpu_custom_call", output_to_operand_aliasing={{0}: (18, {}), {1}: (19, {})} | custom-call | flops 10240000000 | bytes 30000000 | tf_op jit(solution)/shard_map/post_short/pallas_call | solution.py:660
  120.8 0.0 collective-permute-done.1.refs_2_
  120.8 0.0 copy-start.2
  120.8 0.0 collective-permute-done.refs_1_
  120.9 0.0 copy-start
  120.9 0.0 collective-permute-done.2.refs_3_
  120.9 0.0 copy-start.1
  120.9 0.8 copy-done.2
  121.6 0.2 copy-done
  121.9 0.2 copy-done.1
  122.1 5.7 %end_long.1 = (f32[3,128,768]{2,1,0:T(8,128)}, bf16[1536,1536]{1,0:T(8,128)(2,1)}) custom-call(f32[3,128,768]{2,1,0:T(8,128)S(1)} %get-tuple-element.113.refs_0_, bf16[3,144,768]{2,1,0:T(8,128)(2,1)} %copy-done, bf16[3,128,768]{2,1,0:T(8,128)(2,1)} %copy-done.2, bf16[3,144,768]{2,1,0:T(8,128)(2,1)} %copy-done.1, ...), custom_call_target="tpu_custom_call", output_to_operand_aliasing={{1}: (9, {})} | custom-call | flops 921600000 | bytes 10000000 | tf_op jit(solution)/shard_map/end_long/pallas_call | solution.py:710
  127.7 95.6 %weights.1.block = bf16[35328,128]{1,0:T(8,128)(2,1)S(1)} custom-call(bf16[3072,1536]{1,0:T(8,128)(2,1)} %get-tuple-element.135.refs_0_, bf16[1536,6912]{1,0:T(8,128)(2,1)} %get-tuple-element.136.refs_1_, bf16[896,1536]{1,0:T(8,128)(2,1)} %get-tuple-element.137.refs_2_, bf16[1536,768]{1,0:T(8,128)(2,1)} %get-tuple-element.138.refs_3_, ...), custom_call_target="tpu_custom_call" | custom-call | flops 12872318976 | bytes 50000000 | tf_op jit(solution)/shard_map/weights/pallas_call | solution.py:1008
  223.3 9.5 %unpack.1 = (f32[2,384,1536]{2,1,0:T(8,128)}, f32[2,1536,384]{2,1,0:T(8,128)}, f32[768,768]{1,0:T(8,128)}, f32[768,384]{1,0:T(8,128)}, f32[768,1152]{1,0:T(8,128...) custom-call(bf16[35328,128]{1,0:T(8,128)(2,1)S(1)} %weights.1.block), custom_call_target="tpu_custom_call" | custom-call | bytes 27000000 | tf_op jit(solution)/shard_map/unpack/pallas_call | solution.py:1110
Async XLA Ops:
  64.4 56.4 %collective-permute-start.1 = (bf16[3,128,768]{2,1,0:T(8,128)(2,1)}, bf16[3,128,768]{2,1,0:T(8,128)(2,1)S(1)}, u32[]{:S(2)}, u32[]{:S(2)}) collective-permute-start(bf16[3,128,768]{2,1,0:T(8,128)(2,1)} %get-tuple-element.115), channel_id=1, source_target_pairs={{0,2},{1,3},{2,0},{3,1},{4,6},{5,7},{6,4},{7,5},{8,10},{9,11},{10,... | collective-permute-start | bytes 1769480 | tf_op jit(solution)/shard_map/ppermute | solution.py:1189
  65.3 55.6 %collective-permute-start = (bf16[3,144,768]{2,1,0:T(8,128)(2,1)}, bf16[3,144,768]{2,1,0:T(8,128)(2,1)S(1)}, u32[]{:S(2)}, u32[]{:S(2)}) collective-permute-start(bf16[3,144,768]{2,1,0:T(8,128)(2,1)} %get-tuple-element.114), channel_id=1, source_target_pairs={{0,1},{1,0},{2,3},{3,2},{4,5},{5,4},{6,7},{7,6},{8,9},{9,8},{10,11... | collective-permute-start | bytes 1990664 | tf_op jit(solution)/shard_map/ppermute | solution.py:1189
  65.7 55.1 %collective-permute-start.2 = (bf16[3,144,768]{2,1,0:T(8,128)(2,1)}, bf16[3,144,768]{2,1,0:T(8,128)(2,1)S(1)}, u32[]{:S(2)}, u32[]{:S(2)}) collective-permute-start(bf16[3,144,768]{2,1,0:T(8,128)(2,1)} %get-tuple-element.116), channel_id=1, source_target_pairs={{0,3},{1,2},{2,1},{3,0},{4,7},{5,6},{6,5},{7,4},{8,11},{9,10},{10,... | collective-permute-start | bytes 1990664 | tf_op jit(solution)/shard_map/ppermute | solution.py:1189
  120.8 0.8 copy-start.2
  120.9 1.0 copy-start
  120.9 1.2 copy-start.1
where the time goes:
time: 237 us; the launch traced here: 233 us
  Pallas kernels  228 us (96%)
    pallas_call x1, Pallas kernels, weights_call(): pl.pallas_call(functools.partial(weights_body, remote, ((0, 0, n_short),...  95.6 us
    pallas_call x2, Pallas kernels, ffn_call(): pl.pallas_call(functools.partial(ffn_body, slot_rows if masked else 0), g...  45.3 us
    pallas_call x2, Pallas kernels, post_call(): pl.pallas_call(functools.partial(post_body, len(xs)), grid=(count // batc...  37 us
    pallas_call x2, Pallas kernels, pre_call(): pl.pallas_call(functools.partial(pre_body, len(xs)), grid=(count // batch...  35.3 us
    pallas_call x1, Pallas kernels, unpack_call(): pl.pallas_call(unpack_body, grid=(CHUNKS,), in_specs=[pl.BlockSpec((CHUNK...  9.55 us
    pallas_call x1, Pallas kernels, end_call(): pl.pallas_call(functools.partial(end_body, 1 + len(far)), grid=(count,),...  5.65 us
  transfers between devices with their start and end apart: 3, of which 0 were waited for; matrix products, arithmetic and copies ran while one was open for 0% of the time, Pallas kernels for 23%

commit v1 on v0

--- a/solution.py
+++ b/solution.py
@@ -129,18 +129,19 @@
 class Gather:
     def __init__(self, own, outs, send_sem, recv_sem):
         self.own, self.outs, self.send_sem, self.recv_sem = own, outs, send_sem, recv_sem
+        self.rows = own.shape[0]
         dp, blk = lax.axis_index("dp"), lax.axis_index("blk")
         core, x = lax.rem(blk, 2), blk // 2
         self.core_peer = (dp, blk + 1 - 2 * core)
         self.x_peer = (dp, blk + 2 - 4 * x)
 
-    def copy(self, i):
+    def copy(self, i, r):
         source = self.outs[1] if i == 2 else self.own
         return pltpu.make_async_remote_copy(
-            src_ref=source,
-            dst_ref=self.outs[i],
-            send_sem=self.send_sem.at[i],
-            recv_sem=self.recv_sem.at[i],
+            src_ref=source.at[r],
+            dst_ref=self.outs[i].at[r],
+            send_sem=self.send_sem.at[i, r],
+            recv_sem=self.recv_sem.at[i, r],
             device_id=self.x_peer if i == 1 else self.core_peer,
             device_id_type=pl.DeviceIdType.MESH,
         )
@@ -152,18 +153,20 @@
                 barrier, inc=1, device_id=device, device_id_type=pl.DeviceIdType.MESH
             )
         pl.semaphore_wait(barrier, 2)
-        self.copy(1).start()
-        self.copy(0).start()
-
-    def forward(self):
-        self.copy(1).wait_recv()
-        self.copy(2).start()
+        for i in (1, 0):
+            for r in range(self.rows):
+                self.copy(i, r).start()
+
+    def forward(self, r):
+        self.copy(1, r).wait_recv()
+        self.copy(2, r).start()
 
     def end(self):
-        for i in (0, 2):
-            self.copy(i).wait_recv()
-        for i in range(3):
-            self.copy(i).wait_send()
+        for r in range(self.rows):
+            for i in (0, 2):
+                self.copy(i, r).wait_recv()
+            for i in range(3):
+                self.copy(i, r).wait_send()
 
 
 def pre_body(n_x, *refs):
@@ -189,6 +192,13 @@
         vec[8:17, :] = depth_kernel[...].astype(F32)
         if gather:
             gather.begin()
+
+    if gather:
+
+        @pl.when(pl.program_id(0) == pl.num_programs(0) - 1)
+        def _():
+            for r in range(gather.rows - 1):
+                gather.forward(r)
 
     batch, rows = x_refs[0].shape[:2]
     total_rows = batch * rows
@@ -252,7 +262,7 @@
 
         @pl.when(pl.program_id(0) == pl.num_programs(0) - 1)
         def _():
-            gather.forward()
+            gather.forward(gather.rows - 1)
 
     low_half = lane < HEAD
     parts = two_parts(kernel)
@@ -336,9 +346,9 @@
             (in_vmem if not gathered or i == 8 else pltpu.HBM)((count, *s), t)
             for i, (s, t) in enumerate(shapes)
         ]
-        + [pltpu.HBM(g.shape, g.dtype) for g in gathered] * 3,
+        + [in_vmem(g.shape, g.dtype) for g in gathered] * 3,
         scratch_shapes=[pltpu.VMEM((batch, D // 128, rows + 16, 128), F32), pltpu.VMEM((24, D), F32)]
-        + [pltpu.SemaphoreType.DMA((3,))] * (2 * len(gathered)),
+        + [pltpu.SemaphoreType.DMA((3, g.shape[0])) for g in gathered for _ in range(2)],
         compiler_params=params("pre_short", collective_id=1, has_side_effects=True)
         if gathered
         else params("pre_long"),
@@ -346,7 +356,7 @@
             flops=count * rows * 6_000_000, bytes_accessed=20_000_000, transcendentals=1_000_000
         ),
         name="pre_long" if len(xs) > 1 else "pre_short",
-    )(*fetched(*gathered, *xs, *consts))
+    )(*fetched(*gathered, xs[0]), *held(*xs[1:]), *fetched(*consts))
 
 
 def norm_stats(z):
@@ -656,7 +666,7 @@
         pltpu.VMEM((wide, ALL), F32),
     ]
     row_args = held(*row_args) if is_long else held(mg, fig) + fetched(*row_args[2:])
-    inputs = [*fetched(*xs), *row_args, *fetched(*consts)]
+    inputs = [*fetched(xs[0]), *held(*xs[1:]), *row_args, *fetched(*consts)]
     return pl.pallas_call(
         functools.partial(post_body, len(xs)),
         grid=(count // batch,),
@@ -706,7 +716,7 @@
     count, rows = own.shape[0], own.shape[1]
     first = (joint.shape[0] - count * rows) // rows
     (own,), (qt, ug, tg) = held(own), held(qt, ug, tg)
-    row_args = [own, *fetched(*far), qt, ug, tg]
+    row_args = [own, *held(*far), qt, ug, tg]
     return pl.pallas_call(
         functools.partial(end_body, 1 + len(far)),
         grid=(count,),
@@ -738,7 +748,7 @@
 
 
 CHUNK_PARTS = (
-    ((0, 2560, "cxyz"), (2560, 2048, "cyxz")),
+    ((0, 2048, "cyxz"), (2048, 2560, "cxyz")),
     ((4608, 2560, "cxyz"), (7168, 2048, "cyxz")),
     ((9216, 2560, "cxyz"), (11776, 2048, "cyxz")),
     ((13824, 1536, "cxyz"), (15360, 3072, "cyxz")),
@@ -890,26 +900,31 @@
         else:
             a, a_rows, b, b_cols = left_post, (0, D + 128), right_post, (0, D)
         copies = []
-        for i, (to, start, size) in enumerate(ranges):
-            here, there = pl.ds(to, size), pl.ds(start, size)
-            copies.append(
-                pltpu.make_async_copy(
-                    a.at[pl.ds(*a_rows), there],
-                    held_left.at[slot, : a_rows[1], here],
-                    load_sem.at[slot, 2 * i],
+        halves = 2 if k == 0 else 1
+        cols = b_cols[1] // halves
+        for half in range(halves):
+            for i, (to, start, size) in enumerate(ranges):
+                here, there = pl.ds(to, size), pl.ds(start, size)
+                if half == 0:
+                    copies.append(
+                        pltpu.make_async_copy(
+                            a.at[pl.ds(*a_rows), there],
+                            held_left.at[slot, : a_rows[1], here],
+                            load_sem.at[slot, i],
+                        )
+                    )
+                copies.append(
+                    pltpu.make_async_copy(
+                        b.at[there, pl.ds(b_cols[0] + half * cols, cols)],
+                        held_right.at[slot, here, half * cols : (half + 1) * cols],
+                        load_sem.at[slot, 2 + 2 * half + i],
+                    )
                 )
-            )
-            copies.append(
-                pltpu.make_async_copy(
-                    b.at[there, pl.ds(*b_cols)],
-                    held_right.at[slot, here, : b_cols[1]],
-                    load_sem.at[slot, 2 * i + 1],
-                )
-            )
         return copies
 
     def compute(k):
-        for copy in loads(k):
+        coming = loads(k)
+        for copy in coming[:4]:
             copy.wait()
         if k + 1 < CHUNKS:
             for copy in loads(k + 1):
@@ -933,7 +948,14 @@
                 ].astype(BF)
             return carry
 
-        lax.fori_loop(0, 2 if k == 7 else 4, unit, 0)
+        lax.fori_loop(0, 2 if k in (0, 7) else 4, unit, 0)
+        if k == 0:
+            if remote:
+                exchange.await_greetings()
+                exchange.stage(0, 0)
+            for copy in coming[4:]:
+                copy.wait()
+            lax.fori_loop(2, 4, unit, 0)
         ones = jnp.ones((16, tokens), BF)
         if k in (0, 1, 4, 5):
             wide = 2 if k == 4 else 4
@@ -961,6 +983,10 @@
                 ]
             part[SMALL_ROW + 3 * SMALL :, :] = jnp.zeros((PACKED - SMALL_ROW - 3 * SMALL, 128), BF)
 
+    if remote:
+        res, got, *sems = scratch
+        exchange = Exchange(part, res, out, got, sems)
+        exchange.greet()
     for copy in loads(0):
         copy.start()
     sums[...] = jnp.zeros_like(sums)
@@ -969,19 +995,15 @@
             compute(k)
         pltpu.sync_copy(part, out)
         return
-    res, got, *sems = scratch
-    exchange = Exchange(part, res, out, got, sems)
-    exchange.greet()
     for t in range(CHUNKS + 8):
         if t < CHUNKS:
             compute(t)
-        if t == 0:
-            exchange.await_greetings()
         for k in reversed(range(CHUNKS)):
             if 0 <= t - k <= 8:
                 first = sum(len(p) for p in CHUNK_PARTS[:k])
                 for n in range(first, first + len(CHUNK_PARTS[k])):
-                    exchange.stage(n, t - k)
+                    if (n, t) != (0, 0):
+                        exchange.stage(n, t - k)
     exchange.finish()
 
 
@@ -994,7 +1016,7 @@
         pltpu.VMEM((2, tokens, 4 * ALL), BF),
         pltpu.VMEM((SMALL, ALL), F32),
         pltpu.VMEM((PACKED, 128), BF),
-        pltpu.SemaphoreType.DMA((2, 4)),
+        pltpu.SemaphoreType.DMA((2, 6)),
     ]
     if remote:
         scratch += [

time: 237 us -> 233 us (0.983)
  no operation moved by 1% of the time
where the time goes in v1:
time: 233 us; the launch traced here: 230 us
  Pallas kernels  226 us (97%)
    pallas_call x1, Pallas kernels, weights_call(): pl.pallas_call(functools.partial(weights_body, remote, ((0, 0, n_short),...  95.4 us
    pallas_call x2, Pallas kernels, ffn_call(): pl.pallas_call(functools.partial(ffn_body, slot_rows if masked else 0), g...  45.3 us
    pallas_call x2, Pallas kernels, post_call(): pl.pallas_call(functools.partial(post_body, len(xs)), grid=(count // batc...  36.8 us
    pallas_call x2, Pallas kernels, pre_call(): pl.pallas_call(functools.partial(pre_body, len(xs)), grid=(count // batch...  33.9 us
    pallas_call x1, Pallas kernels, unpack_call(): pl.pallas_call(unpack_body, grid=(CHUNKS,), in_specs=[pl.BlockSpec((CHUNK...  9.55 us
    pallas_call x1, Pallas kernels, end_call(): pl.pallas_call(functools.partial(end_body, 1 + len(far)), grid=(count,),...  4.91 us
  transfers between devices with their start and end apart: 3, of which 0 were waited for; matrix products, arithmetic and copies ran while one was open for 0% of the time, Pallas kernels for 23%

profile of v1, /device:TPU:1, one launch (start us, length us, event | category | flops | bytes accessed | tf_op | source)
XLA Modules:
  0.0 229.7 jit_solution(14118955194730763302)
XLA Ops:
  0.7 22.7 %pre_short.1 = (bf16[8,128,384]{2,1,0:T(8,128)(2,1)}, bf16[8,128,384]{2,1,0:T(8,128)(2,1)}, bf16[8,128,384]{2,1,0:T(8,128)(2,1)}, bf16[8,3,256,128]{3,2,1,0:T(8,...) custom-call(bf16[3,128,768]{2,1,0:T(8,128)(2,1)} %refs_0_.6, ...), custom_call_target="tpu_custom_call" | custom-call | flops 6144000000 | bytes 20000000 | tf_op jit(solution)/shard_map/pre_short/pallas_call | solution.py:339
  23.3 11.2 %pre_long.1 = (bf16[3,128,384]{2,1,0:T(8,128)(2,1)S(1)}, bf16[3,512,384]{2,1,0:T(8,128)(2,1)S(1)}, bf16[3,512,384]{2,1,0:T(8,128)(2,1)S(1)}, bf16[3,3,1024,128]{...) custom-call(bf16[3,128,768]{2,1,0:T(8,128)(2,1)} %refs_0_.6, ...), custom_call_target="tpu_custom_call" | custom-call | flops 2304000000 | bytes 20000000 | tf_op jit(solution)/shard_map/pre_long/pallas_call | solution.py:339
  34.5 15.0 %ffn_long.1 = (bf16[1,384,768]{2,1,0:T(8,128)(2,1)}, f32[1,384,768]{2,1,0:T(8,128)S(1)}, bf16[1,384,768]{2,1,0:T(8,128)(2,1)S(1)}, bf16[3072,1536]{1,0:T(8,128)(...) custom-call(bf16[1,384,768]{2,1,0:T(8,128)(2,1)S(1)} %bitcast.21, bf16[1,384,768]{2,1,0:T(8,128)(2,1)} %bitcast.27, ...), custom_call_target="tpu_custom_call" | custom-call | flops 4608000000 | bytes 30000000 | tf_op jit(solution)/shard_map/ffn_long/pallas_call | solution.py:470
  49.6 13.2 %post_long.1 = (bf16[896,1536]{1,0:T(8,128)(2,1)}, bf16[1536,768]{1,0:T(8,128)(2,1)}, f32[72,768]{1,0:T(8,128)}, f32[3,128,768]{2,1,0:T(8,128)S(1)}, bf16[3,144,...) custom-call(bf16[3,128,768]{2,1,0:T(8,128)(2,1)} %refs_0_.6, ...), custom_call_target="tpu_custom_call" | custom-call | flops 3840000000 | bytes 30000000 | tf_op jit(solution)/shard_map/post_long/pallas_call | solution.py:670
  62.8 0.8 collective-permute-start.1
  63.6 0.9 collective-permute-start
  64.5 0.6 collective-permute-start.2
  65.8 30.2 %ffn_short.1 = (bf16[4,256,768]{2,1,0:T(8,128)(2,1)}, f32[4,256,768]{2,1,0:T(8,128)S(1)}, bf16[4,256,768]{2,1,0:T(8,128)(2,1)S(1)}, bf16[3072,1536]{1,0:T(8,128)...) custom-call(s32[1,1]{1,0:T(1,128)S(6)} %copy.61.refs_0_, ...), custom_call_target="tpu_custom_call", output_to_operand_aliasing={{3}: (14, {}), {4}: (15, {})} | custom-call | flops 12288000000 | bytes 30000000 | tf_op jit(solution)/shard_map/ffn_short/pallas_call | solution.py:470
  96.0 23.5 %post_short.1 = (bf16[896,1536]{1,0:T(8,128)(2,1)}, bf16[1536,768]{1,0:T(8,128)(2,1)}, f32[72,768]{1,0:T(8,128)}, f32[8,128,768]{2,1,0:T(8,128)}, bf16[1536,1536]{1,0:T(8,128)(2,1)}) custom-call(bf16[8,128,768]{2,1,0:T(8,128)(2,1)} %bitcast.25, bf16[8,128,768]{2,1,0:T(8,128)(2,1)S(1)} %bitcast.18, ...), custom_call_target="tpu_custom_call", output_to_operand_aliasing={{0}: (18, {}), {1}: (19, {})} | custom-call | flops 10240000000 | bytes 30000000 | tf_op jit(solution)/shard_map/post_short/pallas_call | solution.py:670
  119.5 0.0 collective-permute-done.1.refs_2_
  119.6 0.0 collective-permute-done.refs_1_
  119.6 0.0 collective-permute-done.2.refs_3_
  119.6 4.9 %end_long.1 = (f32[3,128,768]{2,1,0:T(8,128)}, bf16[1536,1536]{1,0:T(8,128)(2,1)}) custom-call(f32[3,128,768]{2,1,0:T(8,128)S(1)} %get-tuple-element.113.refs_0_, bf16[3,144,768]{2,1,0:T(8,128)(2,1)S(1)} %collective-permute-done.refs_1_, bf16[3,128,768]{2,1,0:T(8,128)(2,1)S(1)} %collective-permute-done.1.refs_2_, ...), custom_call_target="tpu_custom_call", output_to_operand_aliasing={{1}: (9, {})} | custom-call | flops 921600000 | bytes 10000000 | tf_op jit(solution)/shard_map/end_long/pallas_call | solution.py:720
  124.5 95.4 %weights.1.block = bf16[35328,128]{1,0:T(8,128)(2,1)S(1)} custom-call(bf16[3072,1536]{1,0:T(8,128)(2,1)} %get-tuple-element.135.refs_0_, bf16[1536,6912]{1,0:T(8,128)(2,1)} %get-tuple-element.136.refs_1_, bf16[896,1536]{1,0:T(8,128)(2,1)} %get-tuple-element.137.refs_2_, bf16[1536,768]{1,0:T(8,128)(2,1)} %get-tuple-element.138.refs_3_, ...), custom_call_target="tpu_custom_call" | custom-call | flops 12872318976 | bytes 50000000 | tf_op jit(solution)/shard_map/weights/pallas_call | solution.py:1030
  219.9 9.5 %unpack.1 = (f32[2,384,1536]{2,1,0:T(8,128)}, f32[2,1536,384]{2,1,0:T(8,128)}, f32[768,768]{1,0:T(8,128)}, f32[768,384]{1,0:T(8,128)}, f32[768,1152]{1,0:T(8,128...) custom-call(bf16[35328,128]{1,0:T(8,128)(2,1)S(1)} %weights.1.block), custom_call_target="tpu_custom_call" | custom-call | bytes 27000000 | tf_op jit(solution)/shard_map/unpack/pallas_call | solution.py:1132
Async XLA Ops:
  62.8 56.7 %collective-permute-start.1 = (bf16[3,128,768]{2,1,0:T(8,128)(2,1)}, bf16[3,128,768]{2,1,0:T(8,128)(2,1)S(1)}, u32[]{:S(2)}, u32[]{:S(2)}) collective-permute-start(bf16[3,128,768]{2,1,0:T(8,128)(2,1)} %get-tuple-element.115), channel_id=1, source_target_pairs={{0,2},{1,3},{2,0},{3,1},{4,6},{5,7},{6,4},{7,5},{8,10},{9,11},{10,... | collective-permute-start | bytes 1769480 | tf_op jit(solution)/shard_map/ppermute | solution.py:1211
  63.6 55.9 %collective-permute-start = (bf16[3,144,768]{2,1,0:T(8,128)(2,1)}, bf16[3,144,768]{2,1,0:T(8,128)(2,1)S(1)}, u32[]{:S(2)}, u32[]{:S(2)}) collective-permute-start(bf16[3,144,768]{2,1,0:T(8,128)(2,1)} %get-tuple-element.114), channel_id=1, source_target_pairs={{0,1},{1,0},{2,3},{3,2},{4,5},{5,4},{6,7},{7,6},{8,9},{9,8},{10,11... | collective-permute-start | bytes 1990664 | tf_op jit(solution)/shard_map/ppermute | solution.py:1211
  64.5 55.0 %collective-permute-start.2 = (bf16[3,144,768]{2,1,0:T(8,128)(2,1)}, bf16[3,144,768]{2,1,0:T(8,128)(2,1)S(1)}, u32[]{:S(2)}, u32[]{:S(2)}) collective-permute-start(bf16[3,144,768]{2,1,0:T(8,128)(2,1)} %get-tuple-element.116), channel_id=1, source_target_pairs={{0,3},{1,2},{2,1},{3,0},{4,7},{5,6},{6,5},{7,4},{8,11},{9,10},{10,... | collective-permute-start | bytes 1990664 | tf_op jit(solution)/shard_map/ppermute | solution.py:1211

commit v2 on v1

--- a/solution.py
+++ b/solution.py
@@ -750,12 +750,12 @@
 CHUNK_PARTS = (
     ((0, 2048, "cyxz"), (2048, 2560, "cxyz")),
     ((4608, 2560, "cxyz"), (7168, 2048, "cyxz")),
-    ((9216, 2560, "cxyz"), (11776, 2048, "cyxz")),
-    ((13824, 1536, "cxyz"), (15360, 3072, "cyxz")),
-    ((18432, 2048, "cyxz"), (20480, 2048, "cxyz"), (22528, 512, "czxy")),
-    ((23040, 2048, "cxyz"), (25088, 1024, "czxy"), (26112, 1536, "cyxz")),
-    ((27648, 1536, "cxyz"), (29184, 1024, "czyx"), (30208, 2048, "cyxz")),
-    ((32256, 1024, "cyxz"), (33280, 1536, "cxyz"), (34816, 512, "cyzx")),
+    ((9216, 3072, "cxyz"), (12288, 1536, "cyxz")),
+    ((13824, 1536, "cyxz"), (15360, 3072, "cxyz")),
+    ((18432, 2048, "cyxz"), (20480, 2560, "cxyz")),
+    ((23040, 2048, "cxyz"), (25088, 2048, "cyzx"), (27136, 512, "czyx")),
+    ((27648, 2560, "cxyz"), (30208, 2048, "cyzx")),
+    ((32256, 1536, "cxyz"), (33792, 1024, "cyzx"), (34816, 512, "cxyz")),
 )
 PARTS = sum(CHUNK_PARTS, ())
 

time: 233 us -> 232 us (level)
  no operation moved by 1% of the time
where the time goes in v2:
time: 232 us; the launch traced here: 229 us
  Pallas kernels  225 us (97%)
    pallas_call x1, Pallas kernels, weights_call(): pl.pallas_call(functools.partial(weights_body, remote, ((0, 0, n_short),...  94.7 us
    pallas_call x2, Pallas kernels, ffn_call(): pl.pallas_call(functools.partial(ffn_body, slot_rows if masked else 0), g...  45.3 us
    pallas_call x2, Pallas kernels, post_call(): pl.pallas_call(functools.partial(post_body, len(xs)), grid=(count // batc...  36.8 us
    pallas_call x2, Pallas kernels, pre_call(): pl.pallas_call(functools.partial(pre_body, len(xs)), grid=(count // batch...  33.9 us
    pallas_call x1, Pallas kernels, unpack_call(): pl.pallas_call(unpack_body, grid=(CHUNKS,), in_specs=[pl.BlockSpec((CHUNK...  9.55 us
    pallas_call x1, Pallas kernels, end_call(): pl.pallas_call(functools.partial(end_body, 1 + len(far)), grid=(count,),...  4.93 us
  transfers between devices with their start and end apart: 3, of which 0 were waited for; matrix products, arithmetic and copies ran while one was open for 0% of the time, Pallas kernels for 23%

profile of v2, /device:TPU:1, one launch (start us, length us, event | category | flops | bytes accessed | tf_op | source)
XLA Modules:
  0.0 229.0 jit_solution(17749528116666835139)
XLA Ops:
  0.7 22.7 %pre_short.1 = (bf16[8,128,384]{2,1,0:T(8,128)(2,1)}, bf16[8,128,384]{2,1,0:T(8,128)(2,1)}, bf16[8,128,384]{2,1,0:T(8,128)(2,1)}, bf16[8,3,256,128]{3,2,1,0:T(8,...) custom-call(bf16[3,128,768]{2,1,0:T(8,128)(2,1)} %refs_0_.6, ...), custom_call_target="tpu_custom_call" | custom-call | flops 6144000000 | bytes 20000000 | tf_op jit(solution)/shard_map/pre_short/pallas_call | solution.py:339
  23.3 11.2 %pre_long.1 = (bf16[3,128,384]{2,1,0:T(8,128)(2,1)S(1)}, bf16[3,512,384]{2,1,0:T(8,128)(2,1)S(1)}, bf16[3,512,384]{2,1,0:T(8,128)(2,1)S(1)}, bf16[3,3,1024,128]{...) custom-call(bf16[3,128,768]{2,1,0:T(8,128)(2,1)} %refs_0_.6, ...), custom_call_target="tpu_custom_call" | custom-call | flops 2304000000 | bytes 20000000 | tf_op jit(solution)/shard_map/pre_long/pallas_call | solution.py:339
  34.5 15.0 %ffn_long.1 = (bf16[1,384,768]{2,1,0:T(8,128)(2,1)}, f32[1,384,768]{2,1,0:T(8,128)S(1)}, bf16[1,384,768]{2,1,0:T(8,128)(2,1)S(1)}, bf16[3072,1536]{1,0:T(8,128)(...) custom-call(bf16[1,384,768]{2,1,0:T(8,128)(2,1)S(1)} %bitcast.21, bf16[1,384,768]{2,1,0:T(8,128)(2,1)} %bitcast.27, ...), custom_call_target="tpu_custom_call" | custom-call | flops 4608000000 | bytes 30000000 | tf_op jit(solution)/shard_map/ffn_long/pallas_call | solution.py:470
  49.6 13.2 %post_long.1 = (bf16[896,1536]{1,0:T(8,128)(2,1)}, bf16[1536,768]{1,0:T(8,128)(2,1)}, f32[72,768]{1,0:T(8,128)}, f32[3,128,768]{2,1,0:T(8,128)S(1)}, bf16[3,144,...) custom-call(bf16[3,128,768]{2,1,0:T(8,128)(2,1)} %refs_0_.6, ...), custom_call_target="tpu_custom_call" | custom-call | flops 3840000000 | bytes 30000000 | tf_op jit(solution)/shard_map/post_long/pallas_call | solution.py:670
  62.8 0.8 collective-permute-start.1
  63.6 0.9 collective-permute-start
  64.5 0.6 collective-permute-start.2
  65.8 30.2 %ffn_short.1 = (bf16[4,256,768]{2,1,0:T(8,128)(2,1)}, f32[4,256,768]{2,1,0:T(8,128)S(1)}, bf16[4,256,768]{2,1,0:T(8,128)(2,1)S(1)}, bf16[3072,1536]{1,0:T(8,128)...) custom-call(s32[1,1]{1,0:T(1,128)S(6)} %copy.61.refs_0_, ...), custom_call_target="tpu_custom_call", output_to_operand_aliasing={{3}: (14, {}), {4}: (15, {})} | custom-call | flops 12288000000 | bytes 30000000 | tf_op jit(solution)/shard_map/ffn_short/pallas_call | solution.py:470
  96.0 23.5 %post_short.1 = (bf16[896,1536]{1,0:T(8,128)(2,1)}, bf16[1536,768]{1,0:T(8,128)(2,1)}, f32[72,768]{1,0:T(8,128)}, f32[8,128,768]{2,1,0:T(8,128)}, bf16[1536,1536]{1,0:T(8,128)(2,1)}) custom-call(bf16[8,128,768]{2,1,0:T(8,128)(2,1)} %bitcast.25, bf16[8,128,768]{2,1,0:T(8,128)(2,1)S(1)} %bitcast.18, ...), custom_call_target="tpu_custom_call", output_to_operand_aliasing={{0}: (18, {}), {1}: (19, {})} | custom-call | flops 10240000000 | bytes 30000000 | tf_op jit(solution)/shard_map/post_short/pallas_call | solution.py:670
  119.5 0.0 collective-permute-done.1.refs_2_
  119.6 0.0 collective-permute-done.refs_1_
  119.6 0.0 collective-permute-done.2.refs_3_
  119.6 4.9 %end_long.1 = (f32[3,128,768]{2,1,0:T(8,128)}, bf16[1536,1536]{1,0:T(8,128)(2,1)}) custom-call(f32[3,128,768]{2,1,0:T(8,128)S(1)} %get-tuple-element.113.refs_0_, bf16[3,144,768]{2,1,0:T(8,128)(2,1)S(1)} %collective-permute-done.refs_1_, bf16[3,128,768]{2,1,0:T(8,128)(2,1)S(1)} %collective-permute-done.1.refs_2_, ...), custom_call_target="tpu_custom_call", output_to_operand_aliasing={{1}: (9, {})} | custom-call | flops 921600000 | bytes 10000000 | tf_op jit(solution)/shard_map/end_long/pallas_call | solution.py:720
  124.5 94.7 %weights.1.block = bf16[35328,128]{1,0:T(8,128)(2,1)S(1)} custom-call(bf16[3072,1536]{1,0:T(8,128)(2,1)} %get-tuple-element.135.refs_0_, bf16[1536,6912]{1,0:T(8,128)(2,1)} %get-tuple-element.136.refs_1_, bf16[896,1536]{1,0:T(8,128)(2,1)} %get-tuple-element.137.refs_2_, bf16[1536,768]{1,0:T(8,128)(2,1)} %get-tuple-element.138.refs_3_, ...), custom_call_target="tpu_custom_call" | custom-call | flops 12872318976 | bytes 50000000 | tf_op jit(solution)/shard_map/weights/pallas_call | solution.py:1030
  219.2 9.5 %unpack.1 = (f32[2,384,1536]{2,1,0:T(8,128)}, f32[2,1536,384]{2,1,0:T(8,128)}, f32[768,768]{1,0:T(8,128)}, f32[768,384]{1,0:T(8,128)}, f32[768,1152]{1,0:T(8,128...) custom-call(bf16[35328,128]{1,0:T(8,128)(2,1)S(1)} %weights.1.block), custom_call_target="tpu_custom_call" | custom-call | bytes 27000000 | tf_op jit(solution)/shard_map/unpack/pallas_call | solution.py:1132
Async XLA Ops:
  62.8 56.7 %collective-permute-start.1 = (bf16[3,128,768]{2,1,0:T(8,128)(2,1)}, bf16[3,128,768]{2,1,0:T(8,128)(2,1)S(1)}, u32[]{:S(2)}, u32[]{:S(2)}) collective-permute-start(bf16[3,128,768]{2,1,0:T(8,128)(2,1)} %get-tuple-element.115), channel_id=1, source_target_pairs={{0,2},{1,3},{2,0},{3,1},{4,6},{5,7},{6,4},{7,5},{8,10},{9,11},{10,... | collective-permute-start | bytes 1769480 | tf_op jit(solution)/shard_map/ppermute | solution.py:1211
  63.6 55.9 %collective-permute-start = (bf16[3,144,768]{2,1,0:T(8,128)(2,1)}, bf16[3,144,768]{2,1,0:T(8,128)(2,1)S(1)}, u32[]{:S(2)}, u32[]{:S(2)}) collective-permute-start(bf16[3,144,768]{2,1,0:T(8,128)(2,1)} %get-tuple-element.114), channel_id=1, source_target_pairs={{0,1},{1,0},{2,3},{3,2},{4,5},{5,4},{6,7},{7,6},{8,9},{9,8},{10,11... | collective-permute-start | bytes 1990664 | tf_op jit(solution)/shard_map/ppermute | solution.py:1211
  64.5 55.0 %collective-permute-start.2 = (bf16[3,144,768]{2,1,0:T(8,128)(2,1)}, bf16[3,144,768]{2,1,0:T(8,128)(2,1)S(1)}, u32[]{:S(2)}, u32[]{:S(2)}) collective-permute-start(bf16[3,144,768]{2,1,0:T(8,128)(2,1)} %get-tuple-element.116), channel_id=1, source_target_pairs={{0,3},{1,2},{2,1},{3,0},{4,7},{5,6},{6,5},{7,4},{8,11},{9,10},{10,... | collective-permute-start | bytes 1990664 | tf_op jit(solution)/shard_map/ppermute | solution.py:1211
